TPU v7x, 32 devices: a whole 2x2x4 slice. The times are simulated.
32 devices in a mesh: dp: 16 (over z, y, core), tensor: 2 (over x).
Axes of the slice: x: 2, y: 2, z: 4, core: 2. Of those that a mesh axis runs over, the one named last changes fastest.
Arguments:
- block_in: bfloat16 [16384, 1024], P(('dp', 'tensor')), may hold values from -6 to 6
- norm_gain: float32 [1024], replicated, may hold values from 0.25 to 1.75
- proj_gate: bfloat16 [1024, 2048], P('dp', 'tensor'), may hold values from -0.1875 to 0.1875
- proj_value: bfloat16 [1024, 2048], P('dp', 'tensor'), may hold values from -0.1875 to 0.1875
- proj_step: bfloat16 [1024, 32], P('dp', 'tensor'), may hold values from -0.1875 to 0.1875
- proj_bc: bfloat16 [1024, 256], P('dp'), may hold values from -0.1875 to 0.1875
- conv_value: float32 [5, 2048], P(None, 'tensor'), may hold values from -2 to 2
- conv_bc: float32 [5, 256], replicated, may hold values from -2 to 2
- head_params: float32 [3, 32], P(None, 'tensor'), may hold values from -6 to 2.5, as said below
- gate_gain: float32 [2048], P('tensor'), may hold values from 0.25 to 1.75
- proj_out: bfloat16 [2048, 1024], P('tensor', 'dp'), may hold values from -0.125 to 0.125
- grad_out: bfloat16 [16384, 1024], P(('dp', 'tensor')), may hold values from -6 to 6
Outputs:
- block_out: bfloat16 [16384, 1024], P(('dp', 'tensor'))
- grad_in: bfloat16 [16384, 1024], P(('dp', 'tensor'))
- grad_norm_gain: float32 [1024], replicated
- grad_proj_gate: float32 [1024, 2048], P('dp', 'tensor')
- grad_proj_value: float32 [1024, 2048], P('dp', 'tensor')
- grad_proj_step: float32 [1024, 32], P('dp', 'tensor')
- grad_proj_bc: float32 [1024, 256], P('dp')
- grad_conv_value: float32 [5, 2048], P(None, 'tensor')
- grad_conv_bc: float32 [5, 256], replicated
- grad_head_params: float32 [3, 32], P(None, 'tensor')
- grad_gate_gain: float32 [2048], P('tensor')
- grad_proj_out: float32 [2048, 1024], P('tensor', 'dp')
Inputs may be any that keep to these rules, and one draw needn't show every extreme that they name: `head_params`: row 0 is added to the step before the softplus, row 1 is the logarithm of the decay rate, row 2 is the skip factor.
All inputs are finite; a program needn't handle non-finite values.
Results may differ from a plain program's by a relative error of at most 0.02.
Values may be sent and summed in bfloat16 or wider, within the bound.
A program may use at most 192 MiB of HBM per device.

v0:
```python
import jax
import jax.numpy as jnp
from jax import lax
from jax.sharding import PartitionSpec as P

SPAN = 256
SEQ_LEN = 1024
INNER = 2048


EPS = 1e-05
MIXER_PRECISION = lax.Precision.HIGH


def causal_conv(signal, kernel_rows):
    extent = kernel_rows.shape[0] - 1
    length = signal.shape[1]
    padded = jnp.pad(signal, ((0, 0), (extent - 1, 0), (0, 0)))
    summed = kernel_rows[extent] + padded[:, 0:length, :] * kernel_rows[0]
    for offset in range(1, extent):
        summed = summed + padded[:, offset : offset + length, :] * kernel_rows[offset]
    return jax.nn.silu(summed)


def convolve(value_raw, bc_raw, conv_value, conv_bc):
    return (causal_conv(value_raw, conv_value), causal_conv(bc_raw, conv_bc))


def mixer(value_conv, bc_conv, step_raw, head_params, gate_raw):
    seq_count, seq_length, chan_count = value_conv.shape
    head_count = step_raw.shape[2]
    head_size = chan_count // head_count
    state_count = bc_conv.shape[2] // 2
    block_count = seq_length // SPAN
    step_size = jax.nn.softplus(step_raw + head_params[0])
    decay_rate = -jnp.exp(head_params[1])
    values = value_conv.reshape(seq_count, block_count, SPAN, head_count, head_size)
    in_keys = bc_conv[..., :state_count].reshape(seq_count, block_count, SPAN, state_count)
    out_reads = bc_conv[..., state_count:].reshape(seq_count, block_count, SPAN, state_count)
    head_steps = jnp.transpose(
        step_size.reshape(seq_count, block_count, SPAN, head_count), (0, 1, 3, 2)
    )
    log_decay = jnp.cumsum(head_steps * decay_rate[:, None], axis=3)
    causal = jnp.arange(SPAN)[:, None] >= jnp.arange(SPAN)[None, :]
    spread = log_decay[..., :, None] - log_decay[..., None, :]
    decay_mat = jnp.where(causal, jnp.exp(jnp.where(causal, spread, 0.0)), 0.0)
    intersection = jnp.einsum("skin,skjn->skij", out_reads, in_keys, precision=MIXER_PRECISION)
    mixing = intersection[:, :, None] * decay_mat * head_steps[..., None, :]
    inside = jnp.einsum("skhij,skjhp->skihp", mixing, values, precision=MIXER_PRECISION)
    tail_weight = jnp.exp(log_decay[..., -1:] - log_decay) * head_steps
    local_state = jnp.einsum(
        "skhj,skjhp,skjn->skhpn", tail_weight, values, in_keys, precision=MIXER_PRECISION
    )
    block_fade = jnp.exp(log_decay[..., -1])

    def advance(carried, inputs):
        local_piece, factor = inputs
        return (carried * factor[..., None, None] + local_piece, carried)

    start_state = jnp.zeros((seq_count, head_count, head_size, state_count), local_state.dtype)
    unused, before = lax.scan(
        advance, start_state, (jnp.moveaxis(local_state, 1, 0), jnp.moveaxis(block_fade, 1, 0))
    )
    before = jnp.moveaxis(before, 0, 1)
    carried_in = jnp.einsum("skin,skhpn->skihp", out_reads, before, precision=MIXER_PRECISION)
    growth = jnp.transpose(jnp.exp(log_decay), (0, 1, 3, 2))[..., None]
    output = inside + carried_in * growth + head_params[2][:, None] * values
    return output.reshape(seq_count, seq_length, chan_count) * jax.nn.silu(gate_raw)


def rounded(matrix):
    return lax.optimization_barrier(matrix.astype(jnp.bfloat16)).astype(jnp.float32)


def lead_contract(left, right):
    return lax.dot_general(
        left, right, (((0,), (0,)), ((), ())), preferred_element_type=jnp.float32
    )


def tail_contract(left, right):
    return lax.dot_general(
        left, right, (((1,), (1,)), ((), ())), preferred_element_type=jnp.float32
    )


def shards(
    block_in,
    norm_gain,
    proj_gate,
    proj_value,
    proj_step,
    proj_bc,
    conv_value,
    conv_bc,
    head_params,
    gate_gain,
    proj_out,
    grad_out,
):
    tensor_count = lax.axis_size("tensor")
    own_rows = block_in.shape[0]
    all_rows = own_rows * tensor_count
    seq_count = all_rows // SEQ_LEN
    first_row = lax.axis_index("tensor") * own_rows
    model_width = block_in.shape[1]
    block_wide = block_in.astype(jnp.float32)
    inverse = lax.rsqrt(jnp.mean(block_wide * block_wide, axis=1, keepdims=True) + EPS)
    normed = (block_wide * inverse * norm_gain).astype(jnp.bfloat16)
    full_gate, full_value, full_step, full_bc, full_out = (
        lax.all_gather(proj_gate, "dp", axis=0, tiled=True),
        lax.all_gather(proj_value, "dp", axis=0, tiled=True),
        lax.all_gather(proj_step, "dp", axis=0, tiled=True),
        lax.all_gather(proj_bc, "dp", axis=0, tiled=True),
        lax.all_gather(proj_out, "dp", axis=1, tiled=True),
    )
    gathered = lax.all_gather(normed, "tensor", axis=0, tiled=True)
    gate_raw = jnp.dot(gathered, full_gate, preferred_element_type=jnp.float32)
    value_raw = jnp.dot(gathered, full_value, preferred_element_type=jnp.float32)
    step_raw = jnp.dot(gathered, full_step, preferred_element_type=jnp.float32)
    bc_raw = jnp.dot(gathered, full_bc, preferred_element_type=jnp.float32)

    def by_sequence(matrix):
        return matrix.reshape(seq_count, SEQ_LEN, matrix.shape[1])

    conv_pair, conv_back = jax.vjp(
        convolve, by_sequence(value_raw), by_sequence(bc_raw), conv_value, conv_bc
    )
    gated_seq, mixer_back = jax.vjp(
        mixer,
        rounded(conv_pair[0]),
        rounded(conv_pair[1]),
        by_sequence(step_raw),
        head_params,
        by_sequence(gate_raw),
    )
    gated = gated_seq.reshape(all_rows, gated_seq.shape[2])
    squares = jnp.sum(gated * gated, axis=1)
    lifted = (gated * gate_gain).astype(jnp.bfloat16)
    total_squares = lax.psum(squares, "tensor")
    scale_all = lax.rsqrt(total_squares / INNER + EPS)
    branch = lax.psum_scatter(
        jnp.dot(lifted, full_out, preferred_element_type=jnp.float32).astype(jnp.bfloat16),
        "tensor",
        scatter_dimension=0,
        tiled=True,
    ).astype(jnp.float32)
    scale = lax.dynamic_slice_in_dim(scale_all, first_row, own_rows, 0)
    block_out = (block_wide + scale[:, None] * branch).astype(jnp.bfloat16)
    cotangent = grad_out.astype(jnp.float32)
    slope_own = -0.5 * scale * scale * scale * jnp.sum(cotangent * branch, axis=1)
    sent = (scale[:, None] * cotangent).astype(jnp.bfloat16)
    branch_grad, slope = (
        lax.all_gather(sent, "tensor", axis=0, tiled=True),
        lax.all_gather(slope_own.astype(jnp.bfloat16), "tensor", axis=0, tiled=True).astype(
            slope_own.dtype
        ),
    )
    full_gate, full_value, full_step, full_bc, full_out = (
        lax.all_gather(proj_gate, "dp", axis=0, tiled=True),
        lax.all_gather(proj_value, "dp", axis=0, tiled=True),
        lax.all_gather(proj_step, "dp", axis=0, tiled=True),
        lax.all_gather(proj_bc, "dp", axis=0, tiled=True),
        lax.all_gather(proj_out, "dp", axis=1, tiled=True),
    )
    gathered = lax.all_gather(normed, "tensor", axis=0, tiled=True)
    grad_out_local = lead_contract(lifted, branch_grad)
    grad_lifted = tail_contract(branch_grad, full_out)
    grad_gate_gain = jnp.sum(grad_lifted * gated, axis=0)
    grad_gated = grad_lifted * gate_gain + 2.0 / INNER * slope[:, None] * gated
    grad_vconv, grad_bcconv, grad_step, grad_heads, grad_gate_raw = mixer_back(
        by_sequence(grad_gated)
    )
    grad_bcconv = lax.psum(grad_bcconv.astype(jnp.bfloat16), "tensor").astype(jnp.float32)
    grad_value_raw, grad_bc_raw, grad_conv_value, grad_conv_bc = conv_back(
        (grad_vconv, grad_bcconv)
    )

    def flat_low(array):
        return array.reshape(all_rows, array.shape[2]).astype(jnp.bfloat16)

    gate_low = flat_low(grad_gate_raw)
    value_low = flat_low(grad_value_raw)
    step_low = flat_low(grad_step)
    bc_low = flat_low(grad_bc_raw)
    summed = tail_contract(gate_low, full_gate)
    summed = summed + tail_contract(value_low, full_value)
    grad_normed = lax.psum_scatter(
        (summed + tail_contract(step_low, full_step)).astype(jnp.bfloat16),
        "tensor",
        scatter_dimension=0,
        tiled=True,
    ).astype(jnp.float32)
    grad_normed = grad_normed + tail_contract(
        lax.dynamic_slice_in_dim(bc_low, first_row, own_rows, 0), full_bc
    )
    grad_gate_w, grad_value_w, grad_step_w, grad_bc_w, grad_out_w = (
        lax.psum_scatter(
            lead_contract(gathered, gate_low).astype(jnp.bfloat16),
            "dp",
            scatter_dimension=0,
            tiled=True,
        ).astype(jnp.float32),
        lax.psum_scatter(
            lead_contract(gathered, value_low).astype(jnp.bfloat16),
            "dp",
            scatter_dimension=0,
            tiled=True,
        ).astype(jnp.float32),
        lax.psum_scatter(
            lead_contract(gathered, step_low).astype(jnp.bfloat16),
            "dp",
            scatter_dimension=0,
            tiled=True,
        ).astype(jnp.float32),
        lax.psum_scatter(
            lead_contract(gathered, bc_low).astype(jnp.bfloat16),
            "dp",
            scatter_dimension=0,
            tiled=True,
        ).astype(jnp.float32),
        lax.psum_scatter(
            grad_out_local.astype(jnp.bfloat16), "dp", scatter_dimension=1, tiled=True
        ).astype(jnp.float32),
    )
    weighted = grad_normed * norm_gain
    own_gain = jnp.sum(grad_normed * block_wide * inverse, axis=0)
    inverse_cubed = inverse * inverse * inverse
    grad_in = (
        cotangent
        + inverse * weighted
        - block_wide
        * inverse_cubed
        * jnp.sum(weighted * block_wide, axis=1, keepdims=True)
        / model_width
    )
    grad_norm_gain = lax.psum(own_gain, ("dp", "tensor"))
    conv_value_sum, gate_gain_sum, heads_sum, conv_bc_sum = lax.psum(
        (grad_conv_value, grad_gate_gain, grad_heads, grad_conv_bc), "dp"
    )
    return (
        block_out,
        grad_in.astype(jnp.bfloat16),
        grad_norm_gain,
        grad_gate_w,
        grad_value_w,
        grad_step_w,
        grad_bc_w,
        conv_value_sum,
        conv_bc_sum,
        heads_sum,
        gate_gain_sum,
        grad_out_w,
    )


def solution(mesh):
    return jax.shard_map(
        shards,
        mesh=mesh,
        in_specs=(
            P(("dp", "tensor"), None),
            P(),
            P("dp", "tensor"),
            P("dp", "tensor"),
            P("dp", "tensor"),
            P("dp", None),
            P(None, "tensor"),
            P(),
            P(None, "tensor"),
            P("tensor"),
            P("tensor", "dp"),
            P(("dp", "tensor"), None),
        ),
        out_specs=(
            P(("dp", "tensor"), None),
            P(("dp", "tensor"), None),
            P(),
            P("dp", "tensor"),
            P("dp", "tensor"),
            P("dp", "tensor"),
            P("dp", None),
            P(None, "tensor"),
            P(),
            P(None, "tensor"),
            P("tensor"),
            P("tensor", "dp"),
        ),
        check_vma=False,
    )
```

profile of v0, /device:TPU:0, one launch (start us, length us, event | category | flops | bytes accessed | tf_op | source)
XLA Modules:
  0.0 801.2 jit_solution(10888558078305848657)
XLA Ops:
  15.7 23.2 %all-gather = bf16[16,64,16]{1,2,0:T(8,128)(2,1)S(1)} all-gather(bf16[1,64,16]{1,2,0:T(8,128)(2,1)S(1)} %bitcast.354), channel_id=1, replica_groups=mesh['dp'=16,'tensor'=2] {'dp'}, dimensions={0}, use_global_device_ids=true | all-gather | bytes 34816 | tf_op jit(solution)/shard_map/all_gather | solution.py:113
  39.8 18.9 %all_gather.32 = bf16[1024,256]{1,0:T(8,128)(2,1)S(1)} all-gather(bf16[64,256]{1,0:T(8,128)(2,1)S(1)} %copy-done.55), channel_id=1, replica_groups=mesh['dp'=16,'tensor'=2] {'dp'}, dimensions={0}, use_global_device_ids=true | all-gather | bytes 557056 | tf_op jit(solution)/shard_map/all_gather | solution.py:114
  78.2 13.8 %all-gather.10.cloned.1.call-done = bf16[1024,1024]{1,0:T(8,128)(2,1)} async-done(((bf16[64,1024]{1,0:T(8,128)(2,1)}), bf16[1024,1024]{1,0:T(8,128)(2,1)}) %all-gather.10.cloned.1.call-update) | async-done | bytes 2097168 | tf_op jit(solution)/shard_map/all_gather | solution.py:112
  111.5 10.1 %while.34 = (s32[]{:T(128)}, f32[1,16,64,128]{3,2,1,0:T(8,128)S(1)}, f32[4,1,16,64,128]{4,3,2,1,0:T(8,128)}, f32[4,1,16,1,1]{2,4,3,1,0:T(1,128)}, f32[4,1,16]{2,...) while((s32[]{:T(128)}, f32[1,16,64,128]{3,2,1,0:T(8,128)S(1)}, ...), condition=%wide.region_4.5_spmd.clone, body=%wide.region_3.4_spmd.clone.sunk | while | flops 524291 | bytes 2623336 | solution.py:61
  121.6 6.9 reshape.690
  128.5 7.7 copy.180
  141.3 10.7 %fusion.30 = f32[1,4,256,16,64]{2,4,3,1,0:T(8,128)} fusion(f32[1,4,256,16,64]{2,4,3,1,0:T(8,128)S(1)} %copy-done.19, f32[4,256,16,64]{1,3,2,0:T(8,128)S(1)} %fusion.63, f32[4,16,256]{2,1,0:T(8,128)S(1)} %copy-done.43, f32[4,16,256]{2,1,0:T(8,128)S(1)} %copy-done.38, f32[4,256,256]{2,1,0:T(8,128)S(1)} %copy-done.22, pred[256,256]{1,0:T(8,128)(4,1)S(1)} %copy-done.41, ...), kind=kOutput, calls=%fused_computation.54 | convolution fusion | flops 1635778560 | bytes 15990848 | tf_op jit(solution)/shard_map/jvp(skhij,skjhp->skihp)/dot_general | solution.py:49
  151.9 8.1 %copy.222 = f32[1,4,256,16,64]{4,3,2,1,0:T(8,128)} copy(f32[1,4,256,16,64]{2,4,3,1,0:T(8,128)} %fusion.30) | data formatting | bytes 8388608 | tf_op jit(solution)/shard_map/jvp()/reshape | solution.py:68
  160.0 7.6 reshape.693
  167.7 9.7 %multiply_reduce_fusion.9 = (f32[1024]{0:T(1024)S(1)}, f32[1024,1024]{1,0:T(8,128)}, f32[1024,1024]{1,0:T(8,128)}) fusion(f32[1024,1024]{1,0:T(8,128)} %reshape.693, bf16[1024,1024]{1,0:T(8,128)(2,1)} %all-gather.8.cloned.1.call-done, bf16[1024,1024]{1,0:T(8,128)(2,1)} %all-gather.12.cloned.1.call-done), kind=kOutput, calls=%fused_computation.68 | convolution fusion | flops 2154822656 | bytes 16781312 | tf_op jit(solution)/shard_map/dot_general | solution.py:118
  177.4 6.7 convolution_convert_fusion.3
  189.1 25.8 %reduce-scatter.10.cloned.1.call-done = bf16[512,1024]{1,0:T(8,128)(2,1)} async-done(((bf16[1024,1024]{1,0:T(8,128)(2,1)}), bf16[512,1024]{1,0:T(8,128)(2,1)}) %reduce-scatter.10.cloned.1.call-update) | async-done | bytes 1048592 | tf_op jit(solution)/shard_map/reduce_scatter | solution.py:142
  223.4 28.2 %all-gather.16.cloned.1.call-done = bf16[1024,1024]{1,0:T(8,128)(2,1)} async-done(((bf16[512,1024]{1,0:T(8,128)(2,1)}), bf16[1024,1024]{1,0:T(8,128)(2,1)}) %all-gather.16.cloned.1.call-update) | async-done | bytes 2097168 | tf_op jit(solution)/shard_map/all_gather | solution.py:154
  251.6 11.9 %multiply_reduce_fusion.3 = (f32[1024]{0:T(1024)}, bf16[1024,1024]{1,0:T(8,128)(2,1)}, f32[1024,1024]{1,0:T(8,128)S(1)}) fusion(f32[1024,1024]{1,0:T(8,128)} %get-tuple-element.366, f32[1024,1024]{1,0:T(8,128)} %get-tuple-element.408, f32[1024,1024]{1,0:T(8,128)} %reshape.693, f32[1024]{0:T(1024)S(1)} %bitcast.331, f32[1024]{0:T(1024)S(1)} %copy-done.72, ...), kind=kOutput, calls=%fused_computation.59 | convolution fusion | flops 2164259840 | bytes 23080960 | tf_op jit(solution)/shard_map/dot_general | solution.py:82
  293.0 7.2 fusion.81
  301.8 12.1 %while.35 = (s32[]{:T(128)}, f32[1,16,64,128]{3,2,1,0:T(8,128)S(1)}, f32[4,1,16,64,128]{4,3,2,1,0:T(8,128)}, f32[4,1,16]{2,1,0:T(1,128)S(1)}, f32[4,1,16,64,128]...) while((s32[]{:T(128)}, ...), condition=%wide.region_11.12_spmd.clone, body=%wide.region_9.11_spmd.clone.sunk | while | flops 786420 | bytes 3147148 | solution.py:61
  320.7 19.8 %fusion.11 = (f32[4,16,256]{2,1,0:T(8,128)S(1)}, f32[4,16,256]{2,1,0:T(8,128)S(1)}, f32[4,16,256]{2,1,0:T(8,128)}, f32[4,256,256]{2,1,0:T(8,128)}) fusion(f32[4,16,256]{2,1,0:T(8,128)S(1)} %copy-done.44, f32[4,16,256]{2,1,0:T(8,128)S(1)} %copy-done.39, f32[4,256,256]{2,1,0:T(8,128)S(1)} %copy-done.23, pred[256,256]{1,0:T(8,128)(4,1)S(1)} %copy-done.42, ...), kind=kOutput, calls=%fused_computation.22 | convolution fusion | flops 1673216000 | bytes 8781824 | tf_op jit(solution)/shard_map/transpose(jvp(skhij,skjhp->skihp))/dot_general | solution.py:49
  340.6 10.9 %bitcast_add_fusion.2 = f32[1,4,256,16,64]{2,4,3,1,0:T(8,128)} fusion(f32[4,256,16,64]{1,3,2,0:T(8,128)S(1)} %convolution_bitcast_fusion, f32[4,256,16,64]{1,0,3,2:T(4,128)S(1)} %copy-done.2, f32[16]{0:T(128)S(1)} %copy-done.81, f32[4,256,16]{1,2,0:T(8,128)S(1)} %copy-done.25, f32[4,16,256]{2,1,0:T(8,128)S(1)} %copy-done.44, ...), kind=kOutput, calls=%fused_computation.52 | convolution fusion | flops 1635778560 | bytes 18088000 | tf_op jit(solution)/shard_map/transpose(jvp(skhij,skjhp->skihp))/dot_general | solution.py:49
  352.5 10.3 %reduce-window.16 = f32[1,4,16,2,128]{4,2,3,1,0:T(8,128)S(1)} reduce-window(f32[1,4,16,2,128]{4,2,3,1,0:T(8,128)S(1)} %copy.198, f32[]{:T(128)} %constant.106.clone.1), window={size=1x1x1x1x128 pad=0_0x0_0x0_0x0_0x0_127}, to_apply=%region_17.18 | reduce-window | flops 2080768 | bytes 131076 | tf_op jit(solution)/shard_map/reduce-window.2
  373.8 8.1 %copy.224 = f32[1,4,256,16,64]{4,3,2,1,0:T(8,128)} copy(f32[1,4,256,16,64]{2,4,3,1,0:T(8,128)} %bitcast_add_fusion.2) | data formatting | bytes 8388608 | tf_op jit(solution)/shard_map/transpose(jvp())/reshape | solution.py:37
  381.9 7.7 reshape.694
  389.6 13.1 %multiply_reduce_fusion.7 = (f32[1024]{0:T(1024)S(1)}, f32[1024]{0:T(1024)}, f32[1024]{0:T(1024)}, f32[1024]{0:T(1024)}, f32[1024]{0:T(1024)}, /*index=5*/f32[1,1024,1024]{2,1,0:T(8,128)}) fusion(f32[1024,1024]{1,0:T(8,128)} %copy-done, f32[1,1024,1024]{2,1,0:T(8,128)} %bitcast.292, f32[1,1024,1024]{2,1,0:T(8,128)} %get-tuple-element.372, ...), kind=kLoop, calls=%fused_computation.63 | loop fusion | flops 18869248 | bytes 20992000 | tf_op jit(solution)/shard_map/transpose(jvp())/reduce_sum | solution.py:21
  411.7 6.3 broadcast_multiply_fusion
  423.8 6.0 convolution_convert_fusion.1
  429.9 6.7 convolution_convert_fusion
  452.8 9.1 %reduce-scatter.22.cloned.1.call-done = bf16[64,16]{1,0:T(8,128)(2,1)} async-done(((bf16[1024,16]{1,0:T(8,128)(2,1)}), bf16[64,16]{1,0:T(8,128)(2,1)}) %reduce-scatter.22.cloned.1.call-update) | async-done | bytes 2064
  463.4 58.4 %all-reduce.27 = (f32[5,1024]{1,0:T(8,128)}, f32[5,256]{1,0:T(8,128)}, f32[3,16]{1,0:T(4,128)}, f32[1024]{0:T(1024)}) all-reduce(f32[5,1024]{1,0:T(8,128)S(1)} %pad_add_fusion.6, f32[5,256]{1,0:T(8,128)S(1)} %pad_add_fusion.7, f32[3,16]{1,0:T(4,128)S(1)} %pad_add_fusion.8, ...), channel_id=1, replica_groups=mesh['dp'=16,'tensor'=2] {'dp'}, use_global_device_ids=true, to_apply=%region_34.35 | all-reduce | flops 7472 | bytes 59776 | tf_op jit(solution)/shard_map/psum | solution.py:238
  523.1 62.4 %reduce-scatter.16.cloned.1.call-done = bf16[64,1024]{1,0:T(8,128)(2,1)} async-done(((bf16[1024,1024]{1,0:T(8,128)(2,1)}), bf16[64,1024]{1,0:T(8,128)(2,1)}) %reduce-scatter.16.cloned.1.call-update) | async-done | bytes 131088 | tf_op jit(solution)/shard_map/reduce_scatter | solution.py:204
  587.2 62.7 %reduce-scatter.20.cloned.1.call-done = bf16[1024,64]{0,1:T(8,128)(2,1)} async-done(((bf16[1024,1024]{0,1:T(8,128)(2,1)}), bf16[1024,64]{0,1:T(8,128)(2,1)}) %reduce-scatter.20.cloned.1.call-update) | async-done | bytes 131088 | tf_op jit(solution)/shard_map/reduce_scatter | solution.py:222
  651.5 63.0 %reduce-scatter.14.cloned.1.call-done = bf16[64,1024]{1,0:T(8,128)(2,1)} async-done(((bf16[1024,1024]{1,0:T(8,128)(2,1)}), bf16[64,1024]{1,0:T(8,128)(2,1)}) %reduce-scatter.14.cloned.1.call-update) | async-done | bytes 131088 | tf_op jit(solution)/shard_map/reduce_scatter | solution.py:198
  716.2 31.5 %reduce-scatter.12.cloned.1.call-done = bf16[512,1024]{1,0:T(8,128)(2,1)} async-done(((bf16[1024,1024]{1,0:T(8,128)(2,1)}), bf16[512,1024]{1,0:T(8,128)(2,1)}) %reduce-scatter.12.cloned.1.call-update) | async-done | bytes 1048592 | tf_op jit(solution)/shard_map/reduce_scatter | solution.py:188
  751.3 39.3 %psum.51 = f32[1024]{0:T(1024)} all-reduce(f32[1024]{0:T(1024)S(1)} %get-tuple-element.313), channel_id=1, replica_groups=mesh['dp'=16,'tensor'=2] {'dp','tensor'}, use_global_device_ids=true, to_apply=%region_24.25 | all-reduce | flops 1024 | bytes 8192 | tf_op jit(solution)/shard_map/psum | solution.py:237
  (341 shorter events, 184.0 us)
Async XLA Ops:
  7.2 31.9 %copy-start.64 = (f32[5,1024]{1,0:T(8,128)S(1)}, f32[5,1024]{1,0:T(8,128)}, u32[]{:S(2)}) copy-start(f32[5,1024]{1,0:T(8,128)} %param.22) | copy-start | bytes 61444
  7.2 32.5 %copy-start.55 = (bf16[64,256]{1,0:T(8,128)(2,1)S(1)}, bf16[64,256]{1,0:T(8,128)(2,1)}, u32[]{:S(2)}) copy-start(bf16[64,256]{1,0:T(8,128)(2,1)} %param.21) | copy-start | bytes 98308
  7.2 51.4 %copy-start.76 = (f32[5,256]{1,0:T(8,128)S(1)}, f32[5,256]{1,0:T(8,128)}, u32[]{:S(2)}) copy-start(f32[5,256]{1,0:T(8,128)} %param.23) | copy-start | bytes 15364
  7.2 51.5 %all-gather.8.cloned.1.call-start = ((), (), s32[]{:S(2)}) async-start(), calls=%async_computation.7 | async-start | bytes 3145728 | tf_op jit(solution)/shard_map/all_gather | solution.py:117
  12.4 79.5 %all-gather.10.cloned.1.call-start = ((), (), s32[]{:S(2)}) async-start(), calls=%async_computation.8 | async-start | bytes 2228224 | tf_op jit(solution)/shard_map/all_gather | solution.py:112
  13.2 154.5 %all-gather.12.cloned.1.call-start = ((), (), s32[]{:S(2)}) async-start(), calls=%async_computation.9 | async-start | bytes 2228224 | tf_op jit(solution)/shard_map/all_gather | solution.py:111
  13.9 163.4 %all-gather.14.cloned.1.call-start = ((), (), s32[]{:S(2)}) async-start(), calls=%async_computation.10 | async-start | bytes 2228224 | tf_op jit(solution)/shard_map/all_gather | solution.py:115
  14.5 200.4 %reduce-scatter.10.cloned.1.call-start = ((), (), s32[]{:S(2)}) async-start(), calls=%async_computation.11 | async-start | bytes 3145728 | tf_op jit(solution)/shard_map/reduce_scatter | solution.py:142
  15.7 55.2 %copy-start.70 = (f32[16]{0:T(128)}, f32[16]{0:T(128)S(1)}, u32[]{:S(2)}) copy-start(f32[16]{0:T(128)S(1)} %get-tuple-element.405) | copy-start | bytes 196
  39.8 56.1 %copy-start.45 = (f32[1,1024]{1,0:T(1,128)}, f32[1,1024]{1,0:T(1,128)S(1)}, u32[]{:S(2)}) copy-start(f32[1,1024]{1,0:T(1,128)S(1)} %get-tuple-element.392) | copy-start | bytes 12292
  39.8 56.1 %copy-start.47 = (f32[1,1024]{1,0:T(1,128)}, f32[1,1024]{1,0:T(1,128)S(1)}, u32[]{:S(2)}) copy-start(f32[1,1024]{1,0:T(1,128)S(1)} %get-tuple-element.393) | copy-start | bytes 12292
  39.8 56.1 %copy-start.49 = (f32[1,1024]{1,0:T(1,128)}, f32[1,1024]{1,0:T(1,128)S(1)}, u32[]{:S(2)}) copy-start(f32[1,1024]{1,0:T(1,128)S(1)} %get-tuple-element.394) | copy-start | bytes 12292
  39.8 56.1 %copy-start.51 = (f32[1,1024]{1,0:T(1,128)}, f32[1,1024]{1,0:T(1,128)S(1)}, u32[]{:S(2)}) copy-start(f32[1,1024]{1,0:T(1,128)S(1)} %get-tuple-element.395) | copy-start | bytes 12292
  73.6 62.6 %copy-start.15 = (bf16[1,1024,128]{2,1,0:T(8,128)(2,1)}, bf16[1,1024,128]{2,1,0:T(8,128)(2,1)S(1)}, u32[]{:S(2)}) copy-start(bf16[1,1024,128]{2,1,0:T(8,128)(2,1)S(1)} %get-tuple-element.388) | copy-start | bytes 786436
  73.6 65.6 %copy-start.26 = (f32[1,4,256,16]{2,3,0,1:T(8,128)}, f32[1,4,256,16]{2,3,0,1:T(8,128)S(1)}, u32[]{:S(2)}) copy-start(f32[1,4,256,16]{2,3,0,1:T(8,128)S(1)} %copy.287) | copy-start | bytes 196612
  76.2 31.1 %copy-start.24 = (f32[4,256,16]{1,2,0:T(8,128)}, f32[4,256,16]{1,2,0:T(8,128)S(1)}, u32[]{:S(2)}) copy-start(f32[4,256,16]{1,2,0:T(8,128)S(1)} %get-tuple-element.411) | copy-start | bytes 196612
  177.4 37.5 %copy-start.9 = (bf16[512,1024]{1,0:T(8,128)(2,1)S(1)}, bf16[512,1024]{1,0:T(8,128)(2,1)}, u32[]{:S(2)}) copy-start(bf16[512,1024]{1,0:T(8,128)(2,1)} %param.27) | copy-start | bytes 3145732
  184.1 67.5 %all-gather.16.cloned.1.call-start = ((), (), s32[]{:S(2)}) async-start(), calls=%async_computation.12 | async-start | bytes 3145728 | tf_op jit(solution)/shard_map/all_gather | solution.py:154
  218.3 187.1 %all-reduce.30.cloned.1.call-start = ((), (), s32[]{:S(2)}) async-start(), calls=%async_computation.14 | async-start | bytes 1048576 | tf_op jit(solution)/shard_map/psum | solution.py:174
  320.6 30.8 %copy-start.28 = (f32[4,256,16]{1,0,2:T(4,128)}, f32[4,256,16]{1,0,2:T(4,128)S(1)}, u32[]{:S(2)}) copy-start(f32[4,256,16]{1,0,2:T(4,128)S(1)} %multiply_reduce_fusion.2) | copy-start | bytes 196612
  373.7 88.2 %reduce-scatter.22.cloned.1.call-start = ((), (), s32[]{:S(2)}) async-start(), calls=%async_computation.19 | async-start | bytes 278528
  405.3 116.4 %reduce-scatter.18.cloned.1.call-start = ((), (), s32[]{:S(2)}) async-start(), calls=%async_computation.17 | async-start | bytes 557056 | tf_op jit(solution)/shard_map/reduce_scatter | solution.py:216
  411.4 174.1 %reduce-scatter.16.cloned.1.call-start = ((), (), s32[]{:S(2)}) async-start(), calls=%async_computation.16 | async-start | bytes 2228224 | tf_op jit(solution)/shard_map/reduce_scatter | solution.py:204
  429.8 220.1 %reduce-scatter.20.cloned.1.call-start = ((), (), s32[]{:S(2)}) async-start(), calls=%async_computation.18 | async-start | bytes 2228224 | tf_op jit(solution)/shard_map/reduce_scatter | solution.py:222
  436.6 277.9 %reduce-scatter.14.cloned.1.call-start = ((), (), s32[]{:S(2)}) async-start(), calls=%async_computation.15 | async-start | bytes 2228224 | tf_op jit(solution)/shard_map/reduce_scatter | solution.py:198
  442.0 305.6 %reduce-scatter.12.cloned.1.call-start = ((), (), s32[]{:S(2)}) async-start(), calls=%async_computation.13 | async-start | bytes 3145728 | tf_op jit(solution)/shard_map/reduce_scatter | solution.py:188
  449.6 298.1 %copy-start.11 = (bf16[512,1024]{1,0:T(8,128)(2,1)S(1)}, bf16[512,1024]{1,0:T(8,128)(2,1)}, u32[]{:S(2)}) copy-start(bf16[512,1024]{1,0:T(8,128)(2,1)} %param.16) | copy-start | bytes 3145732
  449.6 298.0 %copy-start.57 = (f32[512]{0:T(512)S(1)}, f32[512]{0:T(512)}, u32[]{:S(2)}) copy-start(f32[512]{0:T(512)} %copy-done.56) | copy-start | bytes 6148
  449.6 298.0 %copy-start.58 = (f32[1024]{0:T(1024)S(1)}, f32[1024]{0:T(1024)}, u32[]{:S(2)}) copy-start(f32[1024]{0:T(1024)} %param.17) | copy-start | bytes 12292
  451.7 338.9 %copy-start.10 = (bf16[512,1024]{1,0:T(8,128)(2,1)S(1)}, bf16[512,1024]{1,0:T(8,128)(2,1)}, u32[]{:S(2)}) copy-start(bf16[512,1024]{1,0:T(8,128)(2,1)} %param.27) | copy-start | bytes 3145732
  451.7 338.9 %copy-start.21 = (bf16[512,1024]{1,0:T(8,128)(2,1)S(1)}, bf16[512,1024]{1,0:T(8,128)(2,1)}, u32[]{:S(2)}) copy-start(bf16[512,1024]{1,0:T(8,128)(2,1)} %reduce-scatter.10.cloned.1.call-done) | copy-start | bytes 3145732
  451.7 338.9 %copy-start.69 = (f32[512]{0:T(512)S(1)}, f32[512]{0:T(512)}, u32[]{:S(2)}) copy-start(f32[512]{0:T(512)} %get-tuple-element.401) | copy-start | bytes 6148
  (65 other events, 512.1 us)
Sparse Core Ops, SparseCore 0:
  12.6 35.8 all-gather.7
  50.6 41.3 all-gather.9
  94.1 40.1 all-gather.11
  136.3 40.1 all-gather.13
  184.2 30.6 reduce-scatter.9
  218.4 33.1 all-gather.15
  373.8 28.5 all-reduce.29
  406.6 55.3 reduce-scatter.21
  466.1 54.7 reduce-scatter.17
  524.9 60.6 reduce-scatter.15
  589.3 60.5 reduce-scatter.19
  654.0 60.5 reduce-scatter.13
  716.8 30.8 reduce-scatter.11
where the time goes:
time: 813 us; the launch traced here: 801 us
  waiting for transfers between devices  299 us (37%)
  blocking collectives  149 us (18%)
  matrix products  141 us (17%)
  other arithmetic  102 us (13%)
  local copies, waits for them, and re-layouts  94 us (12%)
  between operations  15.2 us (2%)
    reduce_scatter x1, waiting for transfers between devices, shards(): lax.psum_scatter(lead_contract(gathered, gate_low).astype(jnp.bfloat16),...  63 us
    reduce_scatter x1, waiting for transfers between devices, shards(): lax.psum_scatter(grad_out_local.astype(jnp.bfloat16), 'dp', scatter_dimen...  62.7 us
    reduce_scatter x1, waiting for transfers between devices, shards(): lax.psum_scatter(lead_contract(gathered, value_low).astype(jnp.bfloat16),...  62.4 us
    psum x1, blocking collectives, shards(): lax.psum((grad_conv_value, grad_gate_gain, grad_heads, grad_conv_bc), 'dp')  58.4 us
    dot_general x3, matrix products, mixer(): jnp.einsum('skhij,skjhp->skihp', mixing, values, precision=MIXER_PRECISION)  41.4 us
    psum x1, blocking collectives, shards(): grad_norm_gain = lax.psum(own_gain, ('dp', 'tensor'))  39.3 us
    reduce_scatter x1, waiting for transfers between devices, shards(): lax.psum_scatter((summed + tail_contract(step_low, full_step)).astype(jnp...  31.5 us
    reshape x4, local copies, waits for them, and re-layouts, mixer(): value_conv.reshape(seq_count, block_count, SPAN, head_count, head_size)  30.4 us
  transfers between devices with their start and end apart: 13, of which 8 were waited for; matrix products, arithmetic and copies ran while one was open for 23% of the time, Pallas kernels for 0%

commit v1 on v0

v1 whole, which is shorter than its diff:
```python
import jax
import jax.numpy as jnp
from jax import lax
from jax.experimental import pallas as pl
from jax.experimental.pallas import tpu as pltpu
from jax.sharding import PartitionSpec as P

SPAN = 256
SEQ_LEN = 1024
INNER = 2048


EPS = 1e-05
STATE = 128
VMEM_BYTES = 56 * 1024 * 1024


def causal_conv(signal, kernel_rows):
    extent = kernel_rows.shape[0] - 1
    length = signal.shape[1]
    padded = jnp.pad(signal, ((0, 0), (extent - 1, 0), (0, 0)))
    summed = kernel_rows[extent] + padded[:, 0:length, :] * kernel_rows[0]
    for offset in range(1, extent):
        summed = summed + padded[:, offset : offset + length, :] * kernel_rows[offset]
    return jax.nn.silu(summed)


def convolve(value_raw, bc_raw, conv_value, conv_bc):
    return (causal_conv(value_raw, conv_value), causal_conv(bc_raw, conv_bc))


def spread_matrix(head_count, chan_count):
    size = chan_count // head_count
    rows = lax.broadcasted_iota(jnp.int32, (head_count, chan_count), 0)
    cols = lax.broadcasted_iota(jnp.int32, (head_count, chan_count), 1)
    first = rows * size
    return jnp.where((cols >= first) & (cols < first + size), 1.0, 0.0)


def dot(left, right, dims, precision=None):
    return lax.dot_general(
        left, right, (dims, ((), ())), precision=precision, preferred_element_type=jnp.float32
    )


MM = ((1,), (0,))
TM = ((0,), (0,))
MT = ((1,), (1,))
FULL = lax.Precision.HIGHEST


def widen(table, spread):
    high = table.astype(jnp.bfloat16)
    low = (table - high.astype(jnp.float32)).astype(jnp.bfloat16)
    return dot(high, spread, MM) + dot(low, spread, MM)


def causal_mask():
    rows = lax.broadcasted_iota(jnp.int32, (SPAN, SPAN), 0)
    cols = lax.broadcasted_iota(jnp.int32, (SPAN, SPAN), 1)
    return rows >= cols


def scan_forward_kernel(v_ref, b_ref, c_ref, lc_ref, lr_ref, dt_ref, skip_ref, y_ref, s_ref, state):
    head_count, chan_count = lc_ref.shape[1], v_ref.shape[1]
    size = chan_count // head_count
    group = max(1, 128 // size)

    @pl.when(pl.program_id(1) == 0)
    def _():
        state[...] = jnp.zeros_like(state)

    spread_full = spread_matrix(head_count, chan_count)
    spread = spread_full.astype(jnp.bfloat16)
    values = v_ref[...].astype(jnp.float32)
    b, c, lc = b_ref[...], c_ref[...], lc_ref[...]
    start = state[...]
    s_ref[0] = start
    last = lc[SPAN - 1 : SPAN, :]
    stepped = (widen(dt_ref[...], spread) * values).astype(jnp.bfloat16)
    grow = dot(jnp.exp(lc).astype(jnp.bfloat16), spread, MM)
    base = dot(c, start.astype(jnp.bfloat16), MM) * grow + skip_ref[...] * values
    inter = jnp.where(causal_mask(), dot(c, b, MT), 0.0)
    for lead in range(0, head_count, group):
        parts = []
        for h in range(lead, lead + group):
            decay = jnp.exp(jnp.minimum(lc[:, h : h + 1] - lr_ref[h : h + 1, :], 0.0))
            parts.append(
                dot((inter * decay).astype(jnp.bfloat16), stepped[:, h * size : (h + 1) * size], MM)
            )
        lanes = slice(lead * size, (lead + group) * size)
        y_ref[:, lanes] = base[:, lanes] + jnp.concatenate(parts, axis=1)
    tail = dot(jnp.exp(last - lc).astype(jnp.bfloat16), spread, MM)
    weighted = (tail * stepped.astype(jnp.float32)).astype(jnp.bfloat16)
    fade = dot(jnp.exp(last), spread_full, MM, FULL)
    state[...] = start * fade + dot(b, weighted, TM)


def scan_backward_kernel(
    v_ref, b_ref, c_ref, lc_ref, lr_ref, dt_ref, skip_ref, gy_ref, y_ref, s_ref,
    gv_ref, gb_ref, gc_ref, direct_ref, decay_ref, skipped_ref, adjoint,
):
    head_count, chan_count = lc_ref.shape[1], v_ref.shape[1]
    size = chan_count // head_count
    group = max(1, 128 // size)

    @pl.when(pl.program_id(1) == 0)
    def _():
        adjoint[...] = jnp.zeros_like(adjoint)

    spread_full = spread_matrix(head_count, chan_count)
    spread = spread_full.astype(jnp.bfloat16)
    values = v_ref[...].astype(jnp.float32)
    b, c, lc, gy = b_ref[...], c_ref[...], lc_ref[...], gy_ref[...]
    gy_wide = gy.astype(jnp.float32)
    skip = skip_ref[...]
    start = s_ref[0]
    later = adjoint[...]
    later_low = later.astype(jnp.bfloat16)
    last = lc[SPAN - 1 : SPAN, :]
    steps = widen(dt_ref[...], spread)
    stepped = (steps * values).astype(jnp.bfloat16)
    stepped_wide = stepped.astype(jnp.float32)
    grow = dot(jnp.exp(lc).astype(jnp.bfloat16), spread, MM)
    tail = dot(jnp.exp(last - lc).astype(jnp.bfloat16), spread, MM)
    fade = dot(jnp.exp(last), spread_full, MM, FULL)
    grown = (gy_wide * grow).astype(jnp.bfloat16)
    weighted = (tail * stepped_wide).astype(jnp.bfloat16)
    from_later = dot(b, later_low, MM) * tail
    mask = causal_mask()
    inter = jnp.where(mask, dot(c, b, MT), 0.0)
    mixed = jnp.zeros((SPAN, SPAN), jnp.float32)
    pieces = []
    for lead in range(0, head_count, group):
        for h in range(lead, lead + group):
            lanes = slice(h * size, (h + 1) * size)
            decay = jnp.exp(jnp.minimum(lc[:, h : h + 1] - lr_ref[h : h + 1, :], 0.0))
            pieces.append(dot((inter * decay).astype(jnp.bfloat16), gy[:, lanes], TM))
            mixed = mixed + dot(gy[:, lanes], stepped[:, lanes], MT) * decay
    grad_stepped = from_later + jnp.concatenate(pieces, axis=1)
    gv_ref[...] = steps * grad_stepped + skip * gy_wide
    mixed_low = jnp.where(mask, mixed, 0.0).astype(jnp.bfloat16)
    gc_ref[...] = dot(mixed_low, b, MM) + dot(grown, start.astype(jnp.bfloat16), MT)
    gb_ref[...] = dot(mixed_low, c, TM) + dot(weighted, later_low, MT)
    direct_ref[...] = dot(values * grad_stepped, spread_full, MT, FULL)
    skipped_ref[...] = dot(values * gy_wide, spread_full, MT, FULL)
    ends = jnp.sum(later * start, axis=0, keepdims=True) * fade + jnp.sum(
        stepped_wide * from_later, axis=0, keepdims=True
    )
    balance = gy_wide * (y_ref[...] - skip * values) - stepped_wide * grad_stepped
    rows = lax.broadcasted_iota(jnp.int32, balance.shape, 0)
    balance = balance + jnp.where(rows == SPAN - 1, ends, 0.0)
    onward = jnp.where(mask, 1.0, 0.0)
    decay_ref[...] = dot(onward, dot(balance, spread_full, MT, FULL), TM, FULL)
    adjoint[...] = later * fade + dot(c, grown, TM)


def scan_specs(seq_count, block_count, head_count, chan_count, backward):
    def at(s, k):
        return s * block_count + (block_count - 1 - k if backward else k)

    def tall(width):
        return pl.BlockSpec((SPAN, width), lambda s, k: (at(s, k), 0))

    inputs = [
        tall(chan_count),
        pl.BlockSpec((SPAN, STATE), lambda s, k: (at(s, k), 0)),
        pl.BlockSpec((SPAN, STATE), lambda s, k: (at(s, k), 1)),
        tall(head_count),
        pl.BlockSpec((head_count, SPAN), lambda s, k: (0, at(s, k))),
        tall(head_count),
        pl.BlockSpec((1, chan_count), lambda s, k: (0, 0)),
    ]
    states = pl.BlockSpec((1, STATE, chan_count), lambda s, k: (at(s, k), 0, 0))
    return inputs, tall, states


def scan_forward(values, bc, lc, lr, dt, skip):
    rows, chan_count = values.shape
    head_count = dt.shape[1]
    seq_count, block_count = rows // SEQ_LEN, SEQ_LEN // SPAN
    inputs, tall, states = scan_specs(seq_count, block_count, head_count, chan_count, False)
    return pl.pallas_call(
        scan_forward_kernel,
        grid=(seq_count, block_count),
        in_specs=inputs,
        out_specs=[tall(chan_count), states],
        out_shape=[
            jax.ShapeDtypeStruct((rows, chan_count), jnp.float32),
            jax.ShapeDtypeStruct((rows // SPAN, STATE, chan_count), jnp.float32),
        ],
        scratch_shapes=[pltpu.VMEM((STATE, chan_count), jnp.float32)],
        compiler_params=pltpu.CompilerParams(vmem_limit_bytes=VMEM_BYTES),
        cost_estimate=pl.CostEstimate(
            flops=12 * rows * SPAN * chan_count,
            bytes_accessed=14 * rows * chan_count,
            transcendentals=rows * SPAN * head_count,
        ),
        name="scan_forward",
    )(values, bc, bc, lc, lr, dt, skip)


def scan_backward(values, bc, lc, lr, dt, skip, grad_y, y, states_in):
    rows, chan_count = values.shape
    head_count = dt.shape[1]
    seq_count, block_count = rows // SEQ_LEN, SEQ_LEN // SPAN
    inputs, tall, states = scan_specs(seq_count, block_count, head_count, chan_count, True)
    heads = jax.ShapeDtypeStruct((rows, head_count), jnp.float32)
    return pl.pallas_call(
        scan_backward_kernel,
        grid=(seq_count, block_count),
        in_specs=inputs + [tall(chan_count), tall(chan_count), states],
        out_specs=[tall(chan_count), tall(STATE), tall(STATE)] + [tall(head_count)] * 3,
        out_shape=[
            jax.ShapeDtypeStruct((rows, chan_count), jnp.float32),
            jax.ShapeDtypeStruct((rows, STATE), jnp.float32),
            jax.ShapeDtypeStruct((rows, STATE), jnp.float32),
            heads,
            heads,
            heads,
        ],
        scratch_shapes=[pltpu.VMEM((STATE, chan_count), jnp.float32)],
        compiler_params=pltpu.CompilerParams(vmem_limit_bytes=VMEM_BYTES),
        cost_estimate=pl.CostEstimate(
            flops=36 * rows * SPAN * chan_count,
            bytes_accessed=20 * rows * chan_count,
            transcendentals=rows * SPAN * head_count,
        ),
        name="scan_backward",
    )(values, bc, bc, lc, lr, dt, skip, grad_y, y, states_in)


def swap_with(array, axis, bit):
    count = lax.axis_size(axis)
    return lax.ppermute(array, axis, [(i, i ^ bit) for i in range(count)])


def scatter_rows(array, axis):
    count = lax.axis_size(axis)
    here = lax.axis_index(axis)
    width = array.shape[1]
    held = array.astype(jnp.bfloat16).reshape(count, array.shape[0] // count, width)
    bit = 1
    while bit < count:
        pairs = held.reshape(held.shape[0] // 2, 2, *held.shape[1:])
        mine = (here // bit) % 2
        away = lax.dynamic_index_in_dim(pairs, 1 - mine, 1, keepdims=False)
        kept = lax.dynamic_index_in_dim(pairs, mine, 1, keepdims=False)
        summed = kept.astype(jnp.float32) + swap_with(away, axis, bit).astype(jnp.float32)
        bit *= 2
        held = summed.astype(jnp.bfloat16) if bit < count else summed
    return held[0].astype(jnp.float32)


def gather_rows(array, axis):
    count = lax.axis_size(axis)
    here = lax.axis_index(axis)
    rows, width = array.shape
    held = array[None]
    bit = count // 2
    while bit:
        other = swap_with(held, axis, bit)
        first = (here // bit) % 2 == 0
        held = jnp.stack([jnp.where(first, held, other), jnp.where(first, other, held)], axis=1)
        held = held.reshape(-1, rows, width)
        bit //= 2
    return held.reshape(count * rows, width)


def sum_all(array, axis):
    bit = 1
    while bit < lax.axis_size(axis):
        array = array + swap_with(array, axis, bit)
        bit *= 2
    return array


def rounded(matrix):
    return lax.optimization_barrier(matrix.astype(jnp.bfloat16)).astype(jnp.float32)


def lead_contract(left, right):
    return lax.dot_general(
        left, right, (((0,), (0,)), ((), ())), preferred_element_type=jnp.float32
    )


def tail_contract(left, right):
    return lax.dot_general(
        left, right, (((1,), (1,)), ((), ())), preferred_element_type=jnp.float32
    )


def shards(
    block_in,
    norm_gain,
    proj_gate,
    proj_value,
    proj_step,
    proj_bc,
    conv_value,
    conv_bc,
    head_params,
    gate_gain,
    proj_out,
    grad_out,
):
    tensor_count = lax.axis_size("tensor")
    own_rows = block_in.shape[0]
    all_rows = own_rows * tensor_count
    seq_count = all_rows // SEQ_LEN
    first_row = lax.axis_index("tensor") * own_rows
    model_width = block_in.shape[1]
    block_wide = block_in.astype(jnp.float32)
    inverse = lax.rsqrt(jnp.mean(block_wide * block_wide, axis=1, keepdims=True) + EPS)
    normed = (block_wide * inverse * norm_gain).astype(jnp.bfloat16)
    step_count, bc_count = proj_step.shape[1], proj_bc.shape[1]
    narrow = jnp.concatenate(
        [proj_bc, jnp.pad(proj_step, ((0, 0), (0, -step_count % 128)))], axis=1
    )
    full_narrow = gather_rows(narrow, "dp")
    gathered = gather_rows(normed, "tensor")
    full_value = gather_rows(proj_value, "dp")
    full_gate = gather_rows(proj_gate, "dp")
    full_out_t = gather_rows(proj_out.T, "dp")
    full_bc = full_narrow[:, :bc_count]
    full_step = full_narrow[:, bc_count : bc_count + step_count]
    narrow_raw = jnp.dot(gathered, full_narrow, preferred_element_type=jnp.float32)
    bc_raw = narrow_raw[:, :bc_count]
    step_raw = narrow_raw[:, bc_count : bc_count + step_count]
    value_raw = jnp.dot(gathered, full_value, preferred_element_type=jnp.float32)
    gate_raw = jnp.dot(gathered, full_gate, preferred_element_type=jnp.float32)

    def by_sequence(matrix):
        return matrix.reshape(seq_count, SEQ_LEN, matrix.shape[1])

    conv_pair, conv_back = jax.vjp(
        convolve, by_sequence(value_raw), by_sequence(bc_raw), conv_value, conv_bc
    )
    value_conv = conv_pair[0].reshape(all_rows, -1).astype(jnp.bfloat16)
    bc_conv = conv_pair[1].reshape(all_rows, -1).astype(jnp.bfloat16)
    head_size = value_conv.shape[1] // step_count
    step_in = step_raw + head_params[0]
    steps = jax.nn.softplus(step_in)
    rate = -jnp.exp(head_params[1])
    logs = jnp.cumsum((steps * rate).reshape(-1, SPAN, step_count), axis=1)
    logs = logs.reshape(all_rows, step_count)
    scan_inputs = (
        value_conv,
        bc_conv,
        logs,
        logs.T,
        steps,
        jnp.repeat(head_params[2], head_size)[None],
    )
    y, states = scan_forward(*scan_inputs)
    sigma = jax.nn.sigmoid(gate_raw)
    opened = gate_raw * sigma
    gated = y * opened
    squares = jnp.sum(gated * gated, axis=1)
    lifted = (gated * gate_gain).astype(jnp.bfloat16)
    total_squares = lax.psum(squares, "tensor")
    scale_all = lax.rsqrt(total_squares / INNER + EPS)
    branch = scatter_rows(tail_contract(lifted, full_out_t), "tensor")
    scale = lax.dynamic_slice_in_dim(scale_all, first_row, own_rows, 0)
    block_out = (block_wide + scale[:, None] * branch).astype(jnp.bfloat16)
    cotangent = grad_out.astype(jnp.float32)
    slope_own = -0.5 * scale * scale * scale * jnp.sum(cotangent * branch, axis=1)
    sent = (scale[:, None] * cotangent).astype(jnp.bfloat16)
    branch_grad, slope = (
        gather_rows(sent, "tensor"),
        lax.all_gather(slope_own.astype(jnp.bfloat16), "tensor", axis=0, tiled=True).astype(
            slope_own.dtype
        ),
    )
    grad_out_w = scatter_rows(lead_contract(branch_grad, lifted), "dp").T
    grad_lifted = jnp.dot(branch_grad, full_out_t, preferred_element_type=jnp.float32)
    grad_gate_gain = jnp.sum(grad_lifted * gated, axis=0)
    grad_gated = grad_lifted * gate_gain + 2.0 / INNER * slope[:, None] * gated
    grad_y = (grad_gated * opened).astype(jnp.bfloat16)
    gate_low = (grad_gated * y * sigma * (1.0 + gate_raw * (1.0 - sigma))).astype(jnp.bfloat16)
    grad_gate_w = scatter_rows(lead_contract(gathered, gate_low), "dp")
    grad_vconv, grad_b, grad_c, direct, decayed, skipped = scan_backward(
        *scan_inputs, grad_y, y, states
    )
    grad_bcconv = jnp.concatenate([grad_b, grad_c], axis=1)
    bit = 1
    while bit < tensor_count:
        low = lax.optimization_barrier(grad_bcconv.astype(jnp.bfloat16))
        grad_bcconv = low.astype(jnp.float32) + swap_with(low, "tensor", bit).astype(jnp.float32)
        bit *= 2
    grad_step = (direct + rate * decayed) * jax.nn.sigmoid(step_in)
    grad_heads = jnp.stack(
        [
            jnp.sum(grad_step, axis=0),
            jnp.sum(steps * decayed, axis=0) * rate,
            jnp.sum(skipped, axis=0),
        ]
    )
    grad_value_raw, grad_bc_raw, grad_conv_value, grad_conv_bc = conv_back(
        (by_sequence(grad_vconv), by_sequence(grad_bcconv))
    )

    def flat_low(array):
        return array.reshape(all_rows, array.shape[2]).astype(jnp.bfloat16)

    value_low = flat_low(grad_value_raw)
    step_low = grad_step.astype(jnp.bfloat16)
    bc_low = flat_low(grad_bc_raw)
    grad_value_w = scatter_rows(lead_contract(gathered, value_low), "dp")
    narrow_low = jnp.concatenate(
        [bc_low, jnp.pad(step_low, ((0, 0), (0, -step_count % 128)))], axis=1
    )
    grad_narrow_w = scatter_rows(lead_contract(gathered, narrow_low), "dp")
    grad_bc_w = grad_narrow_w[:, :bc_count]
    grad_step_w = grad_narrow_w[:, bc_count : bc_count + step_count]
    summed = tail_contract(gate_low, full_gate)
    summed = summed + tail_contract(value_low, full_value)
    grad_normed = scatter_rows(summed + tail_contract(step_low, full_step), "tensor")
    grad_normed = grad_normed + tail_contract(
        lax.dynamic_slice_in_dim(bc_low, first_row, own_rows, 0), full_bc
    )
    weighted = grad_normed * norm_gain
    own_gain = jnp.sum(grad_normed * block_wide * inverse, axis=0)
    inverse_cubed = inverse * inverse * inverse
    grad_in = (
        cotangent
        + inverse * weighted
        - block_wide
        * inverse_cubed
        * jnp.sum(weighted * block_wide, axis=1, keepdims=True)
        / model_width
    )
    small = (
        grad_conv_value.reshape(-1),
        grad_gate_gain,
        grad_conv_bc.reshape(-1),
        sum_all(own_gain, "tensor"),
        grad_heads.reshape(-1),
    )
    total = sum(part.shape[0] for part in small)
    packed = jnp.pad(jnp.concatenate(small), (0, -total % 1024)).reshape(-1, 128)
    packed = sum_all(packed, "dp").reshape(-1)
    edges = [0]
    for part in small:
        edges.append(edges[-1] + part.shape[0])
    flat = [packed[edges[i] : edges[i + 1]] for i in range(len(small))]
    conv_value_sum = flat[0].reshape(grad_conv_value.shape)
    gate_gain_sum = flat[1]
    conv_bc_sum = flat[2].reshape(grad_conv_bc.shape)
    grad_norm_gain = flat[3]
    heads_sum = flat[4].reshape(grad_heads.shape)
    return (
        block_out,
        grad_in.astype(jnp.bfloat16),
        grad_norm_gain,
        grad_gate_w,
        grad_value_w,
        grad_step_w,
        grad_bc_w,
        conv_value_sum,
        conv_bc_sum,
        heads_sum,
        gate_gain_sum,
        grad_out_w,
    )


def solution(mesh):
    return jax.shard_map(
        shards,
        mesh=mesh,
        in_specs=(
            P(("dp", "tensor"), None),
            P(),
            P("dp", "tensor"),
            P("dp", "tensor"),
            P("dp", "tensor"),
            P("dp", None),
            P(None, "tensor"),
            P(),
            P(None, "tensor"),
            P("tensor"),
            P("tensor", "dp"),
            P(("dp", "tensor"), None),
        ),
        out_specs=(
            P(("dp", "tensor"), None),
            P(("dp", "tensor"), None),
            P(),
            P("dp", "tensor"),
            P("dp", "tensor"),
            P("dp", "tensor"),
            P("dp", None),
            P(None, "tensor"),
            P(),
            P(None, "tensor"),
            P("tensor"),
            P("tensor", "dp"),
        ),
        check_vma=False,
    )
```

time: 813 us -> 396 us (0.49)
  waiting for transfers between devices: 299 us -> 104 us
  blocking collectives: 149 us -> 48 us
  matrix products: 141 us -> 41.1 us
  local copies, waits for them, and re-layouts: 94 us -> 30.7 us
  Pallas kernels: 0 us -> 44.3 us
  starting transfers between devices: 0.91 us -> 42.3 us
  other arithmetic: 102 us -> 77.2 us
  between operations: 15.2 us -> 2.21 us
    reduce_scatter x6 -> x0, waiting for transfers between devices: 245 us -> none  [the longest x1 63 us: shards(): lax.psum_scatter(lead_contract(gathered, gate_low).astype(jnp.bfloat16),...]
    ppermute x0 -> x42, waiting for transfers between devices: none -> 104 us  [swap_with(): return lax.ppermute(array, axis, [(i, i ^ bit) for i in range(count)])]
    psum x2 -> x0, blocking collectives: 97.7 us -> none  [the longest x1 58.4 us: shards(): lax.psum((grad_conv_value, grad_gate_gain, grad_heads, grad_conv_bc), 'dp')]
    dot_general x15 -> x2, matrix products: 82.9 us -> 6.94 us  [the longest x1 5.69 us: shards(): jnp.dot(branch_grad, full_out_t, preferred_element_type=jnp.float32)]
    reshape x12 -> x11, local copies, waits for them, and re-layouts: 58.3 us -> 2.59 us  [the longest x2 1.02 us: shards(): logs = logs.reshape(all_rows, step_count)]
    pallas_call x0 -> x2, Pallas kernels: none -> 44.3 us  [the longest x1 33.8 us: scan_backward(): pl.pallas_call(scan_backward_kernel, grid=(seq_count, block_count), in_sp...]
    ppermute x0 -> x42, starting transfers between devices: none -> 42.3 us  [swap_with(): return lax.ppermute(array, axis, [(i, i ^ bit) for i in range(count)])]
    all_gather x2 -> x0, blocking collectives: 42.1 us -> none  [the longest x1 23.2 us: shards(): lax.all_gather(proj_step, 'dp', axis=0, tiled=True)]
  transfers between devices with their start and end apart: 13 -> 42, of which waited for: 8 -> 21; matrix products, arithmetic and copies ran while one was open for 23% -> 20% of each run, Pallas kernels for 0% -> 0%
where the time goes in v1:
time: 396 us; the launch traced here: 390 us
  waiting for transfers between devices  104 us (26%)
  other arithmetic  77.2 us (19%)
  blocking collectives  48 us (12%)
  Pallas kernels  44.3 us (11%)
  starting transfers between devices  42.3 us (11%)
  matrix products  41.1 us (10%)
  local copies, waits for them, and re-layouts  30.7 us (8%)
    ppermute x42, waiting for transfers between devices, swap_with(): return lax.ppermute(array, axis, [(i, i ^ bit) for i in range(count)])  104 us
    ppermute x42, starting transfers between devices, swap_with(): return lax.ppermute(array, axis, [(i, i ^ bit) for i in range(count)])  42.3 us
    pallas_call x1, Pallas kernels, scan_backward(): pl.pallas_call(scan_backward_kernel, grid=(seq_count, block_count), in_sp...  33.8 us
    psum x1, blocking collectives, shards(): total_squares = lax.psum(squares, 'tensor')  24.4 us
    all_gather x1, blocking collectives, shards(): lax.all_gather(slope_own.astype(jnp.bfloat16), 'tensor', axis=0, tiled=True)  23.6 us
    reduce_sum x2, other arithmetic, causal_conv(): summed = summed + padded[:, offset:offset + length, :] * kernel_rows[offset]  14.6 us
    dot_general x5, matrix products, tail_contract(): lax.dot_general(left, right, (((1,), (1,)), ((), ())), preferred_element_...  13.2 us
    dot_general x4, matrix products, lead_contract(): lax.dot_general(left, right, (((0,), (0,)), ((), ())), preferred_element_...  11.4 us
  transfers between devices with their start and end apart: 42, of which 21 were waited for; matrix products, arithmetic and copies ran while one was open for 20% of the time, Pallas kernels for 0%

profile of v1, /device:TPU:0, one launch (start us, length us, event | category | flops | bytes accessed | tf_op | source)
XLA Modules:
  0.0 390.0 jit_solution(17864650876214748952)
XLA Ops:
  2.3 4.0 %collective-permute-start.5 = (bf16[1,64,384]{2,1,0:T(8,128)(2,1)S(1)}, bf16[1,64,384]{2,1,0:T(8,128)(2,1)S(1)}, u32[]{:S(2)}, u32[]{:S(2)}) collective-permute-start(bf16[1,64,384]{2,1,0:T(8,128)(2,1)S(1)} %fusion.57), channel_id=1, source_target_pairs={{0,16},{2,18},{4,20},{6,22},{8,24},{10,26},{12,28},{14,30},{16,0},... | collective-permute-start | bytes 147464 | tf_op jit(solution)/shard_map/ppermute | solution.py:235
  6.4 2.9 collective-permute-start.1
  15.2 3.2 collective-permute-start.6
  18.5 6.4 %collective-permute-done.1 = bf16[1,64,1024]{2,1,0:T(8,128)(2,1)S(1)} collective-permute-done((bf16[1,64,1024]{2,1,0:T(8,128)(2,1)}, bf16[1,64,1024]{2,1,0:T(8,128)(2,1)S(1)}, u32[]{:S(2)}, u32[]{:S(2)}) %collective-permute-start.1) | collective-permute-done | bytes 131104 | tf_op jit(solution)/shard_map/ppermute | solution.py:235
  32.6 3.0 collective-permute-done.7
  35.9 4.1 %collective-permute-done.10 = bf16[2,64,1024]{2,1,0:T(8,128)(2,1)S(1)} collective-permute-done((bf16[2,64,1024]{2,1,0:T(8,128)(2,1)S(1)}, bf16[2,64,1024]{2,1,0:T(8,128)(2,1)S(1)}, u32[]{:S(2)}, u32[]{:S(2)}) %collective-permute-start.10) | collective-permute-done | bytes 262176 | tf_op jit(solution)/shard_map/ppermute | solution.py:235
  40.0 5.5 %collective-permute-done.14 = bf16[2,64,1024]{2,1,0:T(8,128)(2,1)S(1)} collective-permute-done((bf16[2,64,1024]{2,1,0:T(8,128)(2,1)S(1)}, bf16[2,64,1024]{2,1,0:T(8,128)(2,1)S(1)}, u32[]{:S(2)}, u32[]{:S(2)}) %collective-permute-start.14) | collective-permute-done | bytes 262176 | tf_op jit(solution)/shard_map/ppermute | solution.py:235
  49.9 10.7 %collective-permute-done.15 = bf16[4,64,1024]{2,1,0:T(8,128)(2,1)S(1)} collective-permute-done((bf16[4,64,1024]{2,1,0:T(8,128)(2,1)S(1)}, bf16[4,64,1024]{2,1,0:T(8,128)(2,1)S(1)}, u32[]{:S(2)}, u32[]{:S(2)}) %collective-permute-start.15) | collective-permute-done | bytes 524320 | tf_op jit(solution)/shard_map/ppermute | solution.py:235
  61.9 9.9 %collective-permute-done.11 = bf16[4,64,1024]{2,1,0:T(8,128)(2,1)S(1)} collective-permute-done((bf16[4,64,1024]{2,1,0:T(8,128)(2,1)S(1)}, bf16[4,64,1024]{2,1,0:T(8,128)(2,1)S(1)}, u32[]{:S(2)}, u32[]{:S(2)}) %collective-permute-start.11) | collective-permute-done | bytes 524320 | tf_op jit(solution)/shard_map/ppermute | solution.py:235
  73.2 9.0 %collective-permute-done.3 = bf16[4,64,1024]{2,1,0:T(8,128)(2,1)S(1)} collective-permute-done((bf16[4,64,1024]{2,1,0:T(8,128)(2,1)S(1)}, bf16[4,64,1024]{2,1,0:T(8,128)(2,1)S(1)}, u32[]{:S(2)}, u32[]{:S(2)}) %collective-permute-start.3) | collective-permute-done | bytes 524320 | tf_op jit(solution)/shard_map/ppermute | solution.py:235
  87.7 2.8 reduce-window.6
  96.0 2.4 select_bitcast_fusion.5
  106.1 4.4 %fusion.24 = (bf16[1024,1024]{1,0:T(8,128)(2,1)}, f32[1,1024,1024]{2,1,0:T(8,128)}) fusion(f32[1024,1024]{1,0:T(8,128)S(1)} %fusion.74, f32[1024]{0:T(1024)S(1)} %bitcast.455, f32[1024]{0:T(1024)S(1)} %bitcast.457, f32[1024]{0:T(1024)S(1)} %bitcast.451, f32[1024]{0:T(1024)S(1)} %bitcast.453, f32[1,1024,1024]{2,1,0:T(8,128)S(1)} %bitcast.390, ...), kind=kLoop, calls=%fused_computation.68 | loop fusion | flops 13631488 | bytes 14700544 | tf_op jit(solution)/shard_map/convert_element_type | solution.py:340
  110.6 10.5 %scan_forward.1 = (f32[1024,1024]{1,0:T(8,128)}, f32[4,128,1024]{2,1,0:T(8,128)}) custom-call(bf16[1024,1024]{1,0:T(8,128)(2,1)} %get-tuple-element.106.v_ref, bf16[1024,256]{1,0:T(8,128)(2,1)} %get-tuple-element.104.b_ref.c_ref, bf16[1024,256]{1,0:T(8,128)(2,1)} %get-tuple-element.104.b_ref.c_ref, f32[1024,16]{1,0:T(8,128)} %copy.91.lc_ref, ...), custom_call_target="tpu_custom_call" | custom-call | flops 3221225472 | bytes 14680064 | tf_op jit(solution)/shard_map/scan_forward/pallas_call | solution.py:183
  121.1 7.3 %multiply_reduce_fusion.5 = (f32[1024]{0:T(1024)S(1)}, f32[1024,1024]{1,0:T(8,128)S(1)}, f32[1024,1024]{1,0:T(8,128)}) fusion(f32[1024,1024]{1,0:T(8,128)} %get-tuple-element.20.y_ref, bf16[1024,1024]{1,0:T(8,128)(2,1)S(1)} %bitcast.414, bf16[1024,1024]{1,0:T(8,128)(2,1)S(1)} %bitcast.420), kind=kOutput, calls=%fused_computation.26 | convolution fusion | flops 2154822656 | bytes 16781312 | tf_op jit(solution)/shard_map/dot_general | solution.py:332
  134.7 24.4 %psum.7 = f32[1024]{0:T(1024)S(1)} all-reduce(f32[1024]{0:T(1024)S(1)} %get-tuple-element.100), channel_id=1, replica_groups=mesh['dp'=16,'tensor'=2] {'tensor'}, use_global_device_ids=true, to_apply=%region_4.5 | all-reduce | flops 1024 | bytes 8192 | tf_op jit(solution)/shard_map/psum | solution.py:362
  163.6 23.6 %all-gather = bf16[2,1,512]{2,1,0:T(2,128)(2,1)S(1)} all-gather(bf16[1,1,512]{2,1,0:T(2,128)(2,1)S(1)} %reshape.391), channel_id=1, replica_groups=mesh['dp'=16,'tensor'=2] {'tensor'}, dimensions={0}, use_global_device_ids=true | all-gather | bytes 3072 | tf_op jit(solution)/shard_map/all_gather | solution.py:372
  191.2 3.8 convolution_convert_fusion
  195.9 5.7 %multiply_convert_fusion = (bf16[1024,1024]{1,0:T(8,128)(2,1)}, bf16[1024,1024]{1,0:T(8,128)(2,1)S(1)}, f32[1024]{0:T(1024)S(1)}) fusion(f32[1024,1024]{1,0:T(8,128)S(1)} %copy-done.52, f32[1024,1024]{1,0:T(8,128)S(1)} %copy-done.50, f32[1024]{0:T(1024)S(1)} %bitcast.479, f32[1024]{0:T(1024)S(1)} %copy-done.48, f32[1024,1024]{1,0:T(8,128)S(1)} %copy-done.51, ...), kind=kOutput, calls=%fused_computation.22 | convolution fusion | flops 2166356992 | bytes 20983808 | tf_op jit(solution)/shard_map/dot_general | solution.py:377
  201.6 3.9 convolution_convert_fusion.2
  205.5 4.5 %fusion.76 = f32[1024,1024]{1,0:T(8,128)} fusion(bf16[1024,1024]{1,0:T(8,128)(2,1)S(1)} %get-tuple-element.109, bf16[1024,1024]{1,0:T(8,128)(2,1)S(1)} %bitcast.421), kind=kOutput, calls=%fused_computation.248 | convolution fusion | flops 2147483648 | bytes 8388608 | tf_op jit(solution)/shard_map/dot_general | solution.py:289
  210.0 33.8 %scan_backward.1 = (f32[1024,1024]{1,0:T(8,128)}, f32[1024,128]{1,0:T(8,128)}, f32[1024,128]{1,0:T(8,128)}, f32[1024,16]{1,0:T(8,128)}, f32[1024,16]{1,0:T(8,128)}, /*index=5*/f32[1024,16]{1,0:T(8,128)}) custom-call(bf16[1024,1024]{1,0:T(8,128)(2,1)} %get-tuple-element.106.v_ref, bf16[1024,256]{1,0:T(8,128)(2,1)} %get-tuple-element.104.b_ref.c_ref, ...), custom_call_target="tpu_custom_call" | custom-call | flops 9663676416 | bytes 20971520 | tf_op jit(solution)/shard_map/scan_backward/pallas_call | solution.py:209
  246.7 12.2 %multiply_reduce_fusion.4 = (f32[1024]{0:T(1024)S(1)}, f32[1024]{0:T(1024)S(1)}, f32[1024]{0:T(1024)S(1)}, f32[1024]{0:T(1024)S(1)}, f32[1024]{0:T(1024)S(1)}, /*index=5*/f32[1,1024,1024]{2,1,0:T(8,128)}) fusion(f32[1024,1024]{1,0:T(8,128)} %copy-done, f32[1,1024,1024]{2,1,0:T(8,128)} %bitcast.391, f32[1,1024,1024]{2,1,0:T(8,128)} %get-tuple-element.107, ...), kind=kLoop, calls=%fused_computation.20 | loop fusion | flops 18869248 | bytes 20992000 | tf_op jit(solution)/shard_map/transpose(jvp())/reduce_sum | solution.py:24
  267.0 5.4 %broadcast_multiply_fusion = (f32[1,1024,1024]{2,1,0:T(8,128)S(1)}, f32[1,1024,1024]{2,1,0:T(8,128)}, f32[1,1024,1024]{2,1,0:T(8,128)}, f32[1,1024,1024]{2,1,0:T(8,128)}) fusion(f32[1,1024,1024]{2,1,0:T(8,128)S(1)} %copy-done.3, f32[1024]{0:T(1024)S(1)} %bitcast.456, f32[1024]{0:T(1024)S(1)} %bitcast.454, f32[1024]{0:T(1024)S(1)} %bitcast.452, ...), kind=kLoop, calls=%fused_computation.64 | loop fusion | flops 4194304 | bytes 20987904 | tf_op jit(solution)/shard_map/transpose(jvp())/mul | solution.py:24
  272.4 7.0 %fusion.8 = bf16[1024,1024]{1,0:T(8,128)(2,1)S(1)} fusion(f32[1,1024,1024]{2,1,0:T(8,128)} %get-tuple-element.112, f32[1,1024,1024]{2,1,0:T(8,128)} %get-tuple-element.113, f32[1,1024,1024]{2,1,0:T(8,128)} %get-tuple-element.114, f32[1,1024,1024]{2,1,0:T(8,128)S(1)} %get-tuple-element.111), kind=kLoop, calls=%fused_computation.38 | loop fusion | flops 4194304 | bytes 18874368 | tf_op jit(solution)/shard_map/convert_element_type | solution.py:405
  285.8 2.5 convolution_convert_fusion.1
  307.3 13.6 %collective-permute-done.19 = bf16[1,512,1024]{2,1,0:T(8,128)(2,1)} collective-permute-done((bf16[1,512,1024]{2,1,0:T(8,128)(2,1)}, bf16[1,512,1024]{2,1,0:T(8,128)(2,1)}, u32[]{:S(2)}, u32[]{:S(2)}) %collective-permute-start.19) | collective-permute-done | bytes 1048608 | tf_op jit(solution)/shard_map/ppermute | solution.py:235
  330.0 13.1 %collective-permute-done.23 = f32[72,128]{1,0:T(8,128)S(1)} collective-permute-done((f32[72,128]{1,0:T(8,128)S(1)}, f32[72,128]{1,0:T(8,128)S(1)}, u32[]{:S(2)}, u32[]{:S(2)}) %collective-permute-start.23) | collective-permute-done | bytes 36896 | tf_op jit(solution)/shard_map/ppermute | solution.py:235
  348.6 2.4 fusion.7
  366.2 7.1 %collective-permute-done.40 = bf16[2,64,1024]{2,1,0:T(8,128)(2,1)S(1)} collective-permute-done((bf16[2,64,1024]{2,1,0:T(8,128)(2,1)S(1)}, bf16[2,64,1024]{2,1,0:T(8,128)(2,1)S(1)}, u32[]{:S(2)}, u32[]{:S(2)}) %collective-permute-start.40) | collective-permute-done | bytes 262176 | tf_op jit(solution)/shard_map/ppermute | solution.py:235
  373.5 2.7 collective-permute-done.28
  377.6 3.1 collective-permute-done.32
  (324 shorter events, 132.9 us)
Async XLA Ops:
  2.3 12.9 %collective-permute-start.5 = (bf16[1,64,384]{2,1,0:T(8,128)(2,1)S(1)}, bf16[1,64,384]{2,1,0:T(8,128)(2,1)S(1)}, u32[]{:S(2)}, u32[]{:S(2)}) collective-permute-start(bf16[1,64,384]{2,1,0:T(8,128)(2,1)S(1)} %fusion.57), channel_id=1, source_target_pairs={{0,16},{2,18},{4,20},{6,22},{8,24},{10,26},{12,28},{14,30},{16,0},... | collective-permute-start | bytes 147464 | tf_op jit(solution)/shard_map/ppermute | solution.py:235
  6.3 18.7 %collective-permute-start.13 = (bf16[1,64,1024]{2,1,0:T(8,128)(2,1)}, bf16[1,64,1024]{2,1,0:T(8,128)(2,1)S(1)}, u32[]{:S(2)}, u32[]{:S(2)}) collective-permute-start(bf16[1,64,1024]{2,1,0:T(8,128)(2,1)} %bitcast.449), channel_id=1, source_target_pairs={{0,16},{2,18},{4,20},{6,22},{8,24},{10,26},{12,28},{14,30},{16,0},... | collective-permute-start | bytes 393224 | tf_op jit(solution)/shard_map/ppermute | solution.py:235
  6.4 18.5 %collective-permute-start.1 = (bf16[1,64,1024]{2,1,0:T(8,128)(2,1)}, bf16[1,64,1024]{2,1,0:T(8,128)(2,1)S(1)}, u32[]{:S(2)}, u32[]{:S(2)}) collective-permute-start(bf16[1,64,1024]{2,1,0:T(8,128)(2,1)} %bitcast.448), channel_id=1, source_target_pairs={{0,16},{2,18},{4,20},{6,22},{8,24},{10,26},{12,28},{14,30},{16,0},... | collective-permute-start | bytes 393224 | tf_op jit(solution)/shard_map/ppermute | solution.py:235
  9.2 17.4 %collective-permute-start.9 = (bf16[1,64,1024]{2,1,0:T(8,128)(2,1)}, bf16[1,64,1024]{2,1,0:T(8,128)(2,1)S(1)}, u32[]{:S(2)}, u32[]{:S(2)}) collective-permute-start(bf16[1,64,1024]{2,1,0:T(8,128)(2,1)} %bitcast.450), channel_id=1, source_target_pairs={{0,16},{2,18},{4,20},{6,22},{8,24},{10,26},{12,28},{14,30},{16,0},... | collective-permute-start | bytes 393224 | tf_op jit(solution)/shard_map/ppermute | solution.py:235
  12.4 71.6 %collective-permute-start = (bf16[1,512,1024]{2,1,0:T(8,128)(2,1)S(1)}, bf16[1,512,1024]{2,1,0:T(8,128)(2,1)S(1)}, u32[]{:S(2)}, u32[]{:S(2)}) collective-permute-start(bf16[1,512,1024]{2,1,0:T(8,128)(2,1)S(1)} %fusion.28), channel_id=1, source_target_pairs={{0,1},{1,0},{2,3},{3,2},{4,5},{5,4},{6,7},{7,6},{8,9},{9,8},{10,11... | collective-permute-start | bytes 3145736 | tf_op jit(solution)/shard_map/ppermute | solution.py:235
  15.2 13.5 %collective-permute-start.6 = (bf16[2,64,384]{2,1,0:T(8,128)(2,1)S(1)}, bf16[2,64,384]{2,1,0:T(8,128)(2,1)S(1)}, u32[]{:S(2)}, u32[]{:S(2)}) collective-permute-start(bf16[2,64,384]{2,1,0:T(8,128)(2,1)S(1)} %maximum_bitcast_fusion.3), channel_id=1, source_target_pairs={{0,8},{2,10},{4,12},{6,14},{8,0},{10,2},{12,4},{14,6},{16,24},{18,... | collective-permute-start | bytes 294920 | tf_op jit(solution)/shard_map/ppermute | solution.py:235
  24.9 22.9 %collective-permute-start.2 = (bf16[2,64,1024]{2,1,0:T(8,128)(2,1)S(1)}, bf16[2,64,1024]{2,1,0:T(8,128)(2,1)S(1)}, u32[]{:S(2)}, u32[]{:S(2)}) collective-permute-start(bf16[2,64,1024]{2,1,0:T(8,128)(2,1)S(1)} %maximum_bitcast_fusion), channel_id=1, source_target_pairs={{0,8},{2,10},{4,12},{6,14},{8,0},{10,2},{12,4},{14,6},{16,24},{18,... | collective-permute-start | bytes 786440 | tf_op jit(solution)/shard_map/ppermute | solution.py:235
  30.5 15.0 %collective-permute-start.14 = (bf16[2,64,1024]{2,1,0:T(8,128)(2,1)S(1)}, bf16[2,64,1024]{2,1,0:T(8,128)(2,1)S(1)}, u32[]{:S(2)}, u32[]{:S(2)}) collective-permute-start(bf16[2,64,1024]{2,1,0:T(8,128)(2,1)S(1)} %maximum_bitcast_fusion.2), channel_id=1, source_target_pairs={{0,8},{2,10},{4,12},{6,14},{8,0},{10,2},{12,4},{14,6},{16,24},{18,... | collective-permute-start | bytes 786440 | tf_op jit(solution)/shard_map/ppermute | solution.py:235
  35.8 13.7 %collective-permute-start.8 = (bf16[8,64,384]{2,1,0:T(8,128)(2,1)S(1)}, bf16[8,64,384]{2,1,0:T(8,128)(2,1)S(1)}, u32[]{:S(2)}, u32[]{:S(2)}) collective-permute-start(bf16[8,64,384]{2,1,0:T(8,128)(2,1)S(1)} %bitcast.433), channel_id=1, source_target_pairs={{0,2},{2,0},{4,6},{6,4},{8,10},{10,8},{12,14},{14,12},{16,18},{18,... | collective-permute-start | bytes 1179656 | tf_op jit(solution)/shard_map/ppermute | solution.py:235
  45.8 14.8 %collective-permute-start.15 = (bf16[4,64,1024]{2,1,0:T(8,128)(2,1)S(1)}, bf16[4,64,1024]{2,1,0:T(8,128)(2,1)S(1)}, u32[]{:S(2)}, u32[]{:S(2)}) collective-permute-start(bf16[4,64,1024]{2,1,0:T(8,128)(2,1)S(1)} %bitcast.405), channel_id=1, source_target_pairs={{0,4},{2,6},{4,0},{6,2},{8,12},{10,14},{12,8},{14,10},{16,20},{18,... | collective-permute-start | bytes 1572872 | tf_op jit(solution)/shard_map/ppermute | solution.py:235
  47.4 24.5 %collective-permute-start.11 = (bf16[4,64,1024]{2,1,0:T(8,128)(2,1)S(1)}, bf16[4,64,1024]{2,1,0:T(8,128)(2,1)S(1)}, u32[]{:S(2)}, u32[]{:S(2)}) collective-permute-start(bf16[4,64,1024]{2,1,0:T(8,128)(2,1)S(1)} %bitcast.403), channel_id=1, source_target_pairs={{0,4},{2,6},{4,0},{6,2},{8,12},{10,14},{12,8},{14,10},{16,20},{18,... | collective-permute-start | bytes 1572872 | tf_op jit(solution)/shard_map/ppermute | solution.py:235
  48.0 34.2 %collective-permute-start.3 = (bf16[4,64,1024]{2,1,0:T(8,128)(2,1)S(1)}, bf16[4,64,1024]{2,1,0:T(8,128)(2,1)S(1)}, u32[]{:S(2)}, u32[]{:S(2)}) collective-permute-start(bf16[4,64,1024]{2,1,0:T(8,128)(2,1)S(1)} %bitcast.404), channel_id=1, source_target_pairs={{0,4},{2,6},{4,0},{6,2},{8,12},{10,14},{12,8},{14,10},{16,20},{18,... | collective-permute-start | bytes 1572872 | tf_op jit(solution)/shard_map/ppermute | solution.py:235
  83.5 10.4 %collective-permute-start.4 = (bf16[8,64,1024]{2,1,0:T(8,128)(2,1)}, bf16[8,64,1024]{2,1,0:T(8,128)(2,1)}, u32[]{:S(2)}, u32[]{:S(2)}) collective-permute-start(bf16[8,64,1024]{2,1,0:T(8,128)(2,1)} %bitcast.15), channel_id=1, source_target_pairs={{0,2},{2,0},{4,6},{6,4},{8,10},{10,8},{12,14},{14,12},{16,18},{18,... | collective-permute-start | bytes 3145736 | tf_op jit(solution)/shard_map/ppermute | solution.py:235
  83.5 12.4 %collective-permute-start.12 = (bf16[8,64,1024]{2,1,0:T(8,128)(2,1)}, bf16[8,64,1024]{2,1,0:T(8,128)(2,1)}, u32[]{:S(2)}, u32[]{:S(2)}) collective-permute-start(bf16[8,64,1024]{2,1,0:T(8,128)(2,1)} %bitcast.65), channel_id=1, source_target_pairs={{0,2},{2,0},{4,6},{6,4},{8,10},{10,8},{12,14},{14,12},{16,18},{18,... | collective-permute-start | bytes 3145736 | tf_op jit(solution)/shard_map/ppermute | solution.py:235
  84.0 14.8 %collective-permute-start.16 = (bf16[8,64,1024]{2,1,0:T(8,128)(2,1)}, bf16[8,64,1024]{2,1,0:T(8,128)(2,1)}, u32[]{:S(2)}, u32[]{:S(2)}) collective-permute-start(bf16[8,64,1024]{2,1,0:T(8,128)(2,1)} %bitcast.80), channel_id=1, source_target_pairs={{0,2},{2,0},{4,6},{6,4},{8,10},{10,8},{12,14},{14,12},{16,18},{18,... | collective-permute-start | bytes 3145736 | tf_op jit(solution)/shard_map/ppermute | solution.py:235
  133.2 25.9 %collective-permute-start.17 = (bf16[1,512,1024]{2,1,0:T(8,128)(2,1)}, bf16[1,512,1024]{2,1,0:T(8,128)(2,1)S(1)}, u32[]{:S(2)}, u32[]{:S(2)}) collective-permute-start(bf16[1,512,1024]{2,1,0:T(8,128)(2,1)} %dynamic-slice_bitcast_fusion.4), channel_id=1, source_target_pairs={{0,1},{1,0},{2,3},{3,2},{4,5},{5,4},{6,7},{7,6},{8,9},{9,8},{10,11... | collective-permute-start | bytes 3145736 | tf_op jit(solution)/shard_map/ppermute | solution.py:235
  162.1 25.1 %collective-permute-start.18 = (bf16[1,512,1024]{2,1,0:T(8,128)(2,1)}, bf16[1,512,1024]{2,1,0:T(8,128)(2,1)}, u32[]{:S(2)}, u32[]{:S(2)}) collective-permute-start(bf16[1,512,1024]{2,1,0:T(8,128)(2,1)} %fusion.29), channel_id=1, source_target_pairs={{0,1},{1,0},{2,3},{3,2},{4,5},{5,4},{6,7},{7,6},{8,9},{9,8},{10,11... | collective-permute-start | bytes 3145736 | tf_op jit(solution)/shard_map/ppermute | solution.py:235
  261.4 26.9 %collective-permute-start.20 = (bf16[1024,256]{1,0:T(8,128)(2,1)S(1)}, bf16[1024,256]{1,0:T(8,128)(2,1)}, u32[]{:S(2)}, u32[]{:S(2)}) collective-permute-start(bf16[1024,256]{1,0:T(8,128)(2,1)S(1)} %pad_maximum_fusion.12), channel_id=1, source_target_pairs={{0,1},{1,0},{2,3},{3,2},{4,5},{5,4},{6,7},{7,6},{8,9},{9,8},{10,11... | collective-permute-start | bytes 1572872 | tf_op jit(solution)/shard_map/ppermute | solution.py:235
  265.4 33.5 %collective-permute-start.38 = (bf16[8,64,1024]{2,1,0:T(8,128)(2,1)}, bf16[8,64,1024]{2,1,0:T(8,128)(2,1)}, u32[]{:S(2)}, u32[]{:S(2)}) collective-permute-start(bf16[8,64,1024]{2,1,0:T(8,128)(2,1)} %dynamic-slice_bitcast_fusion), channel_id=1, source_target_pairs={{0,2},{2,0},{4,6},{6,4},{8,10},{10,8},{12,14},{14,12},{16,18},{18,... | collective-permute-start | bytes 3145736 | tf_op jit(solution)/shard_map/ppermute | solution.py:235
  266.5 36.7 %collective-permute-start.26 = (bf16[8,64,1024]{2,1,0:T(8,128)(2,1)}, bf16[8,64,1024]{2,1,0:T(8,128)(2,1)}, u32[]{:S(2)}, u32[]{:S(2)}) collective-permute-start(bf16[8,64,1024]{2,1,0:T(8,128)(2,1)} %dynamic-slice_bitcast_fusion.2), channel_id=1, source_target_pairs={{0,2},{2,0},{4,6},{6,4},{8,10},{10,8},{12,14},{14,12},{16,18},{18,... | collective-permute-start | bytes 3145736 | tf_op jit(solution)/shard_map/ppermute | solution.py:235
  294.9 28.8 %collective-permute-start.30 = (bf16[8,64,1024]{2,1,0:T(8,128)(2,1)}, bf16[8,64,1024]{2,1,0:T(8,128)(2,1)}, u32[]{:S(2)}, u32[]{:S(2)}) collective-permute-start(bf16[8,64,1024]{2,1,0:T(8,128)(2,1)} %dynamic-slice_bitcast_fusion.1), channel_id=1, source_target_pairs={{0,2},{2,0},{4,6},{6,4},{8,10},{10,8},{12,14},{14,12},{16,18},{18,... | collective-permute-start | bytes 3145736 | tf_op jit(solution)/shard_map/ppermute | solution.py:235
  295.4 25.4 %collective-permute-start.19 = (bf16[1,512,1024]{2,1,0:T(8,128)(2,1)}, bf16[1,512,1024]{2,1,0:T(8,128)(2,1)}, u32[]{:S(2)}, u32[]{:S(2)}) collective-permute-start(bf16[1,512,1024]{2,1,0:T(8,128)(2,1)} %dynamic-slice_bitcast_fusion.3), channel_id=1, source_target_pairs={{0,1},{1,0},{2,3},{3,2},{4,5},{5,4},{6,7},{7,6},{8,9},{9,8},{10,11... | collective-permute-start | bytes 3145736 | tf_op jit(solution)/shard_map/ppermute | solution.py:235
  297.3 32.6 %collective-permute-start.35 = (bf16[4,64,384]{2,1,0:T(8,128)(2,1)S(1)}, bf16[4,64,384]{2,1,0:T(8,128)(2,1)S(1)}, u32[]{:S(2)}, u32[]{:S(2)}) collective-permute-start(bf16[4,64,384]{2,1,0:T(8,128)(2,1)S(1)} %dynamic-slice_bitcast_fusion.12), channel_id=1, source_target_pairs={{0,4},{2,6},{4,0},{6,2},{8,12},{10,14},{12,8},{14,10},{16,20},{18,... | collective-permute-start | bytes 589832 | tf_op jit(solution)/shard_map/ppermute | solution.py:235
  302.6 57.0 %collective-permute-start.39 = (bf16[4,64,1024]{2,1,0:T(8,128)(2,1)}, bf16[4,64,1024]{2,1,0:T(8,128)(2,1)}, u32[]{:S(2)}, u32[]{:S(2)}) collective-permute-start(bf16[4,64,1024]{2,1,0:T(8,128)(2,1)} %dynamic-slice_bitcast_fusion.5), channel_id=1, source_target_pairs={{0,4},{2,6},{4,0},{6,2},{8,12},{10,14},{12,8},{14,10},{16,20},{18,... | collective-permute-start | bytes 1572872 | tf_op jit(solution)/shard_map/ppermute | solution.py:235
  306.1 55.4 %collective-permute-start.27 = (bf16[4,64,1024]{2,1,0:T(8,128)(2,1)}, bf16[4,64,1024]{2,1,0:T(8,128)(2,1)}, u32[]{:S(2)}, u32[]{:S(2)}) collective-permute-start(bf16[4,64,1024]{2,1,0:T(8,128)(2,1)} %dynamic-slice_bitcast_fusion.7), channel_id=1, source_target_pairs={{0,4},{2,6},{4,0},{6,2},{8,12},{10,14},{12,8},{14,10},{16,20},{18,... | collective-permute-start | bytes 1572872 | tf_op jit(solution)/shard_map/ppermute | solution.py:235
  327.8 36.8 %collective-permute-start.31 = (bf16[4,64,1024]{2,1,0:T(8,128)(2,1)}, bf16[4,64,1024]{2,1,0:T(8,128)(2,1)}, u32[]{:S(2)}, u32[]{:S(2)}) collective-permute-start(bf16[4,64,1024]{2,1,0:T(8,128)(2,1)} %dynamic-slice_bitcast_fusion.6), channel_id=1, source_target_pairs={{0,4},{2,6},{4,0},{6,2},{8,12},{10,14},{12,8},{14,10},{16,20},{18,... | collective-permute-start | bytes 1572872 | tf_op jit(solution)/shard_map/ppermute | solution.py:235
  329.3 13.8 %collective-permute-start.23 = (f32[72,128]{1,0:T(8,128)S(1)}, f32[72,128]{1,0:T(8,128)S(1)}, u32[]{:S(2)}, u32[]{:S(2)}) collective-permute-start(f32[72,128]{1,0:T(8,128)S(1)} %fusion.67), channel_id=1, source_target_pairs={{0,4},{2,6},{4,0},{6,2},{8,12},{10,14},{12,8},{14,10},{16,20},{18,... | collective-permute-start | bytes 110600 | tf_op jit(solution)/shard_map/ppermute | solution.py:235
  361.2 12.1 %collective-permute-start.40 = (bf16[2,64,1024]{2,1,0:T(8,128)(2,1)S(1)}, bf16[2,64,1024]{2,1,0:T(8,128)(2,1)S(1)}, u32[]{:S(2)}, u32[]{:S(2)}) collective-permute-start(bf16[2,64,1024]{2,1,0:T(8,128)(2,1)S(1)} %dynamic-slice_bitcast_fusion.9), channel_id=1, source_target_pairs={{0,8},{2,10},{4,12},{6,14},{8,0},{10,2},{12,4},{14,6},{16,24},{18,... | collective-permute-start | bytes 786440 | tf_op jit(solution)/shard_map/ppermute | solution.py:235
  362.8 13.4 %collective-permute-start.28 = (bf16[2,64,1024]{2,1,0:T(8,128)(2,1)S(1)}, bf16[2,64,1024]{2,1,0:T(8,128)(2,1)S(1)}, u32[]{:S(2)}, u32[]{:S(2)}) collective-permute-start(bf16[2,64,1024]{2,1,0:T(8,128)(2,1)S(1)} %dynamic-slice_bitcast_fusion.11), channel_id=1, source_target_pairs={{0,8},{2,10},{4,12},{6,14},{8,0},{10,2},{12,4},{14,6},{16,24},{18,... | collective-permute-start | bytes 786440 | tf_op jit(solution)/shard_map/ppermute | solution.py:235
  365.9 14.9 %collective-permute-start.32 = (bf16[2,64,1024]{2,1,0:T(8,128)(2,1)S(1)}, bf16[2,64,1024]{2,1,0:T(8,128)(2,1)S(1)}, u32[]{:S(2)}, u32[]{:S(2)}) collective-permute-start(bf16[2,64,1024]{2,1,0:T(8,128)(2,1)S(1)} %dynamic-slice_bitcast_fusion.10), channel_id=1, source_target_pairs={{0,8},{2,10},{4,12},{6,14},{8,0},{10,2},{12,4},{14,6},{16,24},{18,... | collective-permute-start | bytes 786440 | tf_op jit(solution)/shard_map/ppermute | solution.py:235
  373.4 11.5 %collective-permute-start.41 = (bf16[1,64,1024]{2,1,0:T(8,128)(2,1)S(1)}, bf16[1,64,1024]{2,1,0:T(8,128)(2,1)S(1)}, u32[]{:S(2)}, u32[]{:S(2)}) collective-permute-start(bf16[1,64,1024]{2,1,0:T(8,128)(2,1)S(1)} %constant_dynamic-slice_fusion), channel_id=1, source_target_pairs={{0,16},{2,18},{4,20},{6,22},{8,24},{10,26},{12,28},{14,30},{16,0},... | collective-permute-start | bytes 393224 | tf_op jit(solution)/shard_map/ppermute | solution.py:235
  376.3 10.0 %collective-permute-start.29 = (bf16[1,64,1024]{2,1,0:T(8,128)(2,1)S(1)}, bf16[1,64,1024]{2,1,0:T(8,128)(2,1)S(1)}, u32[]{:S(2)}, u32[]{:S(2)}) collective-permute-start(bf16[1,64,1024]{2,1,0:T(8,128)(2,1)S(1)} %constant_dynamic-slice_fusion.3), channel_id=1, source_target_pairs={{0,16},{2,18},{4,20},{6,22},{8,24},{10,26},{12,28},{14,30},{16,0},... | collective-permute-start | bytes 393224 | tf_op jit(solution)/shard_map/ppermute | solution.py:235
  (63 other events, 538.2 us)
